TPU v7x, 32 devices: a whole 2x2x4 slice. The times are simulated.
32 devices in a mesh: tm: 8 (over z, y), space: 4 (over x, core).
Axes of the slice: x: 2, y: 2, z: 4, core: 2. Of those that a mesh axis runs over, the one named last changes fastest.
Arguments:
- inverse_factor: bfloat16 [2, 8, 4096, 4096], P(None, 'tm', 'space'), may hold values from -1.5 to 1.5, as said below
- tile_mask: int32 [32, 32], replicated, may hold values 0 or 1
- carry_rate: float32 [8, 4096, 2], P('tm', 'space'), may hold values from 0 to 1
- right_side: float32 [8, 4096, 2, 128], P('tm', 'space'), may hold values from -1.5 to 1.5
- arrow_rows: bfloat16 [8, 4096, 2, 512], P('tm', 'space'), may hold values from -0.125 to 0.125
- fixed_rhs: float32 [2, 512, 128], P(None, ('tm', 'space')), may hold values from -6 to 6
- tip_factor: bfloat16 [2, 512, 512], replicated, may hold values from -1 to 1, as said below
Outputs:
- solution: float32 [8, 4096, 2, 128], P('tm', 'space')
- fixed_solution: float32 [2, 512, 128], P(None, ('tm', 'space'))
Inputs may be any that keep to these rules, and one draw needn't show every extreme that they name: `tile_mask`: 1 marks a tile that may be nonzero. `inverse_factor`: only entries on or below the diagonal are read. `tip_factor`: only entries on or below the diagonal are read.
All inputs are finite; a program needn't handle non-finite values.
Results may differ from a plain program's by a relative error of at most 0.022.
Values may be sent and summed in bfloat16 or wider, within the bound.
A program may use at most 320 MiB of HBM per device.

v0:
```python
import jax
import jax.numpy as jnp
from jax import lax
from jax.sharding import PartitionSpec as P

TILE = 128


def carried_in(shard, axis, join, neutral, backward):
    count = lax.axis_size(axis)
    place = lax.axis_index(axis)
    ahead = count - 1 - place if backward else place
    gathered = jax.tree.map(
        lambda a, kind: lax.all_gather(a.astype(kind), axis), shard, (jnp.bfloat16, jnp.bfloat16)
    )
    state = jax.tree.map(lambda a, e: jnp.zeros_like(a) + jnp.asarray(e, a.dtype), shard, neutral)

    def one(turn, state):
        source = count - 1 - turn if backward else turn
        return join(
            state,
            jax.tree.map(
                lambda a, own: lax.dynamic_index_in_dim(a, source, 0, False).astype(own.dtype),
                gathered,
                shard,
            ),
        )

    return lax.fori_loop(0, ahead, one, state)


def combine(earlier, latter):
    rate_new = latter[0] * earlier[0]
    rest = tuple(
        (value_l + latter[0] * value_e for value_l, value_e in zip(latter[1:], earlier[1:]))
    )
    return (rate_new,) + rest


def tile_keep(tile_table, row_start, row_total, col_total):
    tile_count = tile_table.shape[0]
    tile_ids = jnp.arange(tile_count, dtype=jnp.int32)
    row_index = row_start + jnp.arange(row_total, dtype=jnp.int32)
    col_index = jnp.arange(col_total, dtype=jnp.int32)
    row_onehot = (row_index[:, None] // TILE == tile_ids[None, :]).astype(jnp.float32)
    col_onehot = (col_index[:, None] // TILE == tile_ids[None, :]).astype(jnp.float32)
    marked = jnp.dot(jnp.dot(row_onehot, tile_table.astype(jnp.float32)), col_onehot.T)
    return (marked > 0.5) & (row_index[:, None] >= col_index[None, :])


def on_device(inverse_factor, tile_mask, carry_rate, right_side, arrow_rows, fixed_rhs, tip_factor):
    row_count = right_side.shape[1]
    node_total = inverse_factor.shape[3]
    row_start = lax.axis_index("space") * row_count
    tile_table = jnp.maximum(tile_mask, jnp.eye(tile_mask.shape[0], dtype=jnp.int32))
    weights = inverse_factor[:, 0]
    bf_zero = jnp.zeros((), jnp.bfloat16)
    rate_col = carry_rate[0][:, :, None]
    source = right_side[0]
    unit_rate = jnp.ones_like(rate_col)
    earlier_sum = carried_in(
        (rate_col, source), "tm", combine, (unit_rate, jnp.zeros_like(source)), False
    )
    forward = source + rate_col * earlier_sum[1]
    forward_b = forward.astype(jnp.bfloat16)
    row_keep = tile_keep(tile_table, row_start, row_count, node_total)
    masked_rows = jnp.where(row_keep[None], weights, bf_zero)
    block = masked_rows
    inner_rows = jnp.einsum(
        "hrn,nhk->rhk",
        block,
        lax.all_gather(forward_b, "space", axis=0, tiled=True),
        preferred_element_type=jnp.float32,
    ).astype(jnp.bfloat16)
    block = masked_rows
    scaled = lax.psum_scatter(
        jnp.einsum("hrn,rhk->nhk", block, inner_rows, preferred_element_type=jnp.float32).astype(
            jnp.bfloat16
        ),
        "space",
        scatter_dimension=0,
        tiled=True,
    ).astype(jnp.float32)
    arrow_part = arrow_rows[0]
    coupling = jnp.einsum("rhf,rhk->hfk", arrow_part, forward_b, preferred_element_type=jnp.float32)
    share_rows = fixed_rhs.shape[1]
    share_start = lax.axis_index(("tm", "space")) * share_rows
    contrib = -coupling
    own_part = lax.dynamic_slice_in_dim(contrib, share_start, share_rows, 1) + fixed_rhs
    contrib = lax.dynamic_update_slice_in_dim(contrib, own_part, share_start, 1)
    fixed_forward = lax.psum(contrib, ("tm", "space")).astype(jnp.bfloat16)
    fixed_total = tip_factor.shape[1]
    fixed_index = jnp.arange(fixed_total, dtype=jnp.int32)
    lower_tri = fixed_index[:, None] >= fixed_index[None, :]
    tip_lower = jnp.where(lower_tri[None], tip_factor, bf_zero)
    tip_inner = jnp.einsum(
        "hij,hjk->hik", tip_lower, fixed_forward, preferred_element_type=jnp.float32
    ).astype(jnp.bfloat16)
    fixed_solution = jnp.einsum(
        "hij,hik->hjk", tip_lower, tip_inner, preferred_element_type=jnp.float32
    )
    fixed_own = lax.dynamic_slice_in_dim(fixed_solution, share_start, share_rows, 1)
    fixed_b = fixed_solution.astype(jnp.bfloat16)
    carried = scaled - jnp.einsum(
        "rhf,hfk->rhk", arrow_part, fixed_b, preferred_element_type=jnp.float32
    )
    following = carried_in(
        (rate_col, rate_col * carried), "tm", combine, (unit_rate, jnp.zeros_like(carried)), True
    )
    solution = carried + following[1]
    return (solution[None], fixed_own)


def solution(mesh):
    placed = (
        P(None, "tm", "space", None),
        P(),
        P("tm", "space", None),
        P("tm", "space", None, None),
        P("tm", "space", None, None),
        P(None, ("tm", "space"), None),
        P(),
    )
    return jax.shard_map(
        on_device,
        mesh=mesh,
        in_specs=placed,
        out_specs=(P("tm", "space", None, None), P(None, ("tm", "space"), None)),
        check_vma=False,
    )
```

profile of v0, /device:TPU:0, one launch (start us, length us, event | category | flops | bytes accessed | tf_op | source)
XLA Modules:
  0.0 391.8 jit_solution(15583484226363401883)
XLA Ops:
  7.2 0.0 all-gather.6.cloned.1.call-start
  7.2 2.2 copy.68
  9.5 0.0 all-gather.6.cloned.1.call-update
  9.5 0.0 all-gather.8.cloned.1.call-start
  9.6 2.3 copy.34
  11.8 32.5 %all-gather = bf16[8,1024,2]{1,2,0:T(2,128)(2,1)S(1)} all-gather(bf16[1,1024,2]{1,2,0:T(2,128)(2,1)S(1)} %convert_element_type.103), channel_id=2, replica_groups=mesh['tm'=8,'space'=4] {'tm'}, dimensions={0}, use_global_device_ids=true | all-gather | bytes 36864 | tf_op jit(solution)/shard_map/all_gather | solution.py:14
  44.4 1.8 copy.37
  46.2 40.3 %all-gather.6.cloned.1.call-done = bf16[8,1024,2,128]{3,1,2,0:T(8,128)(2,1)} async-done(((bf16[1,1024,2,128]{3,1,2,0:T(8,128)(2,1)}), bf16[8,1024,2,128]{3,1,2,0:T(8,128)(2,1)}) %all-gather.6.cloned.1.call-update) | async-done | bytes 4194320 | tf_op jit(solution)/shard_map/all_gather | solution.py:14
  86.5 0.3 broadcast.91.clone
  86.8 1.3 copy.38
  88.1 2.5 fusion.25
  90.6 0.0 all-gather.8.cloned.1.call-update
  90.6 0.0 reduce-scatter.2.cloned.1.call-start
  90.7 6.8 %fusion = pred[1024,4096]{1,0:T(8,128)(4,1)} fusion(s32[1024]{0:T(1024)S(1)} %get-tuple-element.186, s32[4096]{0:T(1024)S(1)} %add_select_fusion, s32[1024]{0:T(1024)S(1)} %get-tuple-element.185, s32[32,32]{1,0:T(8,128)S(1)} %copy-done.4), kind=kOutput, calls=%fused_computation.8 | convolution fusion | flops 283283456 | bytes 4222976 | tf_op jit(solution)/shard_map/dot_general | solution.py:47
  97.6 87.4 %all-gather.8.cloned.1.call-done = bf16[4096,2,128]{0,2,1:T(8,128)(2,1)} async-done(((bf16[1024,2,128]{0,2,1:T(8,128)(2,1)}), bf16[4096,2,128]{0,2,1:T(8,128)(2,1)}) %all-gather.8.cloned.1.call-update) | async-done | bytes 2097168 | tf_op jit(solution)/shard_map/all_gather | solution.py:72
  185.0 22.0 %fusion.6 = bf16[4096,2,128]{0,2,1:T(8,128)(2,1)} fusion(bf16[2,1,1024,4096]{3,2,1,0:T(8,128)(2,1)} %param.11, pred[1024,4096]{1,0:T(8,128)(4,1)} %fusion, bf16[4096,2,128]{0,2,1:T(8,128)(2,1)} %all-gather.8.cloned.1.call-done), kind=kOutput, calls=%fused_computation.14 | convolution fusion | flops 4313055232 | bytes 25165824 | tf_op jit(solution)/shard_map/hrn,rhk->nhk/dot_general | solution.py:77
  207.0 0.0 all-gather.10.cloned.1.call-start
  207.1 0.1 copy.40
  207.2 0.8 iota_compare_fusion.1
  208.0 0.4 fusion.18
  208.4 0.1 bitcast_add_fusion.1
  208.5 0.7 dynamic_update_slice.3
  209.2 46.9 %all-reduce.1 = bf16[2,512,128]{1,2,0:T(8,128)(2,1)S(1)} all-reduce(f32[2,512,128]{1,2,0:T(8,128)S(1)} %dynamic_update_slice.3), channel_id=1, replica_groups=mesh['tm'=8,'space'=4] {'tm','space'}, use_global_device_ids=true, to_apply=%region_3.4 | all-reduce | flops 131072 | bytes 786432 | tf_op jit(solution)/shard_map/psum | solution.py:91
  256.1 2.4 fusion.22
  258.6 0.0 reduce-scatter.2.cloned.1.call-done
  258.6 3.0 multiply_convert_fusion
  261.6 0.6 constant_dynamic-slice_fusion.1
  262.3 71.2 %all-gather.10.cloned.1.call-done = bf16[8192,2,128]{0,2,1:T(8,128)(2,1)} async-done(((bf16[1024,2,128]{0,2,1:T(8,128)(2,1)}), bf16[8192,2,128]{0,2,1:T(8,128)(2,1)}) %all-gather.10.cloned.1.call-update) | async-done | bytes 4194320 | tf_op jit(solution)/shard_map/all_gather | solution.py:14
  333.5 11.1 %copy.52 = bf16[8192,2,128]{2,1,0:T(2,128)(2,1)} copy(bf16[8192,2,128]{0,2,1:T(8,128)(2,1)} %all-gather.10.cloned.1.call-done) | data formatting | bytes 8388608 | tf_op jit(solution)/shard_map/while | solution.py:29
  344.6 0.3 broadcast.91
  344.9 36.1 %while.27 = (s32[]{:T(128)}, f32[1024,2,128]{2,1,0:T(2,128)S(1)}, s32[]{:T(128)}, bf16[8,1024,2,128]{3,2,1,0:T(2,128)(2,1)}, bf16[8,1024,2,1]{2,1,3,0:T(8,128)(2...) while((s32[]{:T(128)}, f32[1024,2,128]{2,1,0:T(2,128)S(1)}, s32[]{:T(128)}, ...), condition=%wide.region_5.6_spmd, body=%wide.region_4.5_spmd.sunk | while | flops 788486 | bytes 2642067 | solution.py:29
  344.9 1.0 bitcast_convert_fusion.5
  345.9 4.1 %convert_add_fusion.5 = f32[1024,2,128]{2,1,0:T(2,128)S(1)} fusion(f32[1024,2,128]{2,1,0:T(2,128)S(1)} %get-tuple-element.285, f32[1024,2]{1,0:T(8,128)S(1)} %bitcast_convert_fusion.5, bf16[8,1024,2,128]{3,2,1,0:T(2,128)(2,1)} %get-tuple-element.296, s32[]{:T(128)S(6)} %select_n.78), kind=kLoop, calls=%fused_computation.4.clone.1 | loop fusion | flops 786432 | bytes 2629636 | tf_op jit(solution)/shard_map/while/body/add | solution.py:35
  350.1 1.0 bitcast_convert_fusion.5
  351.1 4.1 %convert_add_fusion.5 = f32[1024,2,128]{2,1,0:T(2,128)S(1)} fusion(f32[1024,2,128]{2,1,0:T(2,128)S(1)} %get-tuple-element.285, f32[1024,2]{1,0:T(8,128)S(1)} %bitcast_convert_fusion.5, bf16[8,1024,2,128]{3,2,1,0:T(2,128)(2,1)} %get-tuple-element.296, s32[]{:T(128)S(6)} %select_n.78), kind=kLoop, calls=%fused_computation.4.clone.1 | loop fusion | flops 786432 | bytes 2629636 | tf_op jit(solution)/shard_map/while/body/add | solution.py:35
  355.2 1.0 bitcast_convert_fusion.5
  356.2 4.1 %convert_add_fusion.5 = f32[1024,2,128]{2,1,0:T(2,128)S(1)} fusion(f32[1024,2,128]{2,1,0:T(2,128)S(1)} %get-tuple-element.285, f32[1024,2]{1,0:T(8,128)S(1)} %bitcast_convert_fusion.5, bf16[8,1024,2,128]{3,2,1,0:T(2,128)(2,1)} %get-tuple-element.296, s32[]{:T(128)S(6)} %select_n.78), kind=kLoop, calls=%fused_computation.4.clone.1 | loop fusion | flops 786432 | bytes 2629636 | tf_op jit(solution)/shard_map/while/body/add | solution.py:35
  360.4 1.0 bitcast_convert_fusion.5
  361.4 4.1 %convert_add_fusion.5 = f32[1024,2,128]{2,1,0:T(2,128)S(1)} fusion(f32[1024,2,128]{2,1,0:T(2,128)S(1)} %get-tuple-element.285, f32[1024,2]{1,0:T(8,128)S(1)} %bitcast_convert_fusion.5, bf16[8,1024,2,128]{3,2,1,0:T(2,128)(2,1)} %get-tuple-element.296, s32[]{:T(128)S(6)} %select_n.78), kind=kLoop, calls=%fused_computation.4.clone.1 | loop fusion | flops 786432 | bytes 2629636 | tf_op jit(solution)/shard_map/while/body/add | solution.py:35
  365.5 1.0 bitcast_convert_fusion.5
  366.5 4.1 %convert_add_fusion.5 = f32[1024,2,128]{2,1,0:T(2,128)S(1)} fusion(f32[1024,2,128]{2,1,0:T(2,128)S(1)} %get-tuple-element.285, f32[1024,2]{1,0:T(8,128)S(1)} %bitcast_convert_fusion.5, bf16[8,1024,2,128]{3,2,1,0:T(2,128)(2,1)} %get-tuple-element.296, s32[]{:T(128)S(6)} %select_n.78), kind=kLoop, calls=%fused_computation.4.clone.1 | loop fusion | flops 786432 | bytes 2629636 | tf_op jit(solution)/shard_map/while/body/add | solution.py:35
  370.7 1.0 bitcast_convert_fusion.5
  371.7 4.1 %convert_add_fusion.5 = f32[1024,2,128]{2,1,0:T(2,128)S(1)} fusion(f32[1024,2,128]{2,1,0:T(2,128)S(1)} %get-tuple-element.285, f32[1024,2]{1,0:T(8,128)S(1)} %bitcast_convert_fusion.5, bf16[8,1024,2,128]{3,2,1,0:T(2,128)(2,1)} %get-tuple-element.296, s32[]{:T(128)S(6)} %select_n.78), kind=kLoop, calls=%fused_computation.4.clone.1 | loop fusion | flops 786432 | bytes 2629636 | tf_op jit(solution)/shard_map/while/body/add | solution.py:35
  375.8 1.0 bitcast_convert_fusion.5
  376.8 4.1 %convert_add_fusion.5 = f32[1024,2,128]{2,1,0:T(2,128)S(1)} fusion(f32[1024,2,128]{2,1,0:T(2,128)S(1)} %get-tuple-element.285, f32[1024,2]{1,0:T(8,128)S(1)} %bitcast_convert_fusion.5, bf16[8,1024,2,128]{3,2,1,0:T(2,128)(2,1)} %get-tuple-element.296, s32[]{:T(128)S(6)} %select_n.78), kind=kLoop, calls=%fused_computation.4.clone.1 | loop fusion | flops 786432 | bytes 2629636 | tf_op jit(solution)/shard_map/while/body/add | solution.py:35
  381.0 1.3 copy.47
  382.3 1.7 add_bitcast_fusion
  384.0 1.3 copy.48
  (16 shorter events, 0.1 us)
Async XLA Ops:
  7.2 200.8 %copy-start = (bf16[1,1024,2,512]{3,2,1,0:T(2,128)(2,1)S(1)}, bf16[1,1024,2,512]{3,2,1,0:T(2,128)(2,1)}, u32[]{:S(2)}) copy-start(bf16[1,1024,2,512]{3,2,1,0:T(2,128)(2,1)} %param.15) | copy-start | bytes 6291460
  7.2 4.6 %copy-start.2 = (f32[1,1024,2]{1,2,0:T(2,128)S(1)}, f32[1,1024,2]{1,2,0:T(2,128)}, u32[]{:S(2)}) copy-start(f32[1,1024,2]{1,2,0:T(2,128)} %param.13) | copy-start | bytes 24580
  7.2 79.3 %all-gather.6.cloned.1.call-start = ((), (), s32[]{:S(2)}) async-start(), calls=%async_computation.1 | async-start | bytes 4718592 | tf_op jit(solution)/shard_map/all_gather | solution.py:14
  9.5 175.5 %all-gather.8.cloned.1.call-start = ((), (), s32[]{:S(2)}) async-start(), calls=%async_computation.2 | async-start | bytes 2621440 | tf_op jit(solution)/shard_map/all_gather | solution.py:72
  86.8 4.0 %copy-start.4 = (s32[32,32]{1,0:T(8,128)S(1)}, s32[32,32]{1,0:T(8,128)}, u32[]{:S(2)}) copy-start(s32[32,32]{1,0:T(8,128)} %param.12) | copy-start | bytes 12292
  90.6 167.9 %reduce-scatter.2.cloned.1.call-start = ((), (), s32[]{:S(2)}) async-start(), calls=%async_computation.3 | async-start | bytes 2621440 | tf_op jit(solution)/shard_map/reduce_scatter | solution.py:76
  97.5 109.5 %copy-start.3 = (f32[2,16,128]{2,1,0:T(8,128)S(1)}, f32[2,16,128]{2,1,0:T(8,128)}, u32[]{:S(2)}) copy-start(f32[2,16,128]{2,1,0:T(8,128)} %param.16) | copy-start | bytes 49156
  97.5 110.4 %copy-start.1 = (bf16[1024,2,128]{0,2,1:T(8,128)(2,1)S(1)}, bf16[1024,2,128]{0,2,1:T(8,128)(2,1)}, u32[]{:S(2)}) copy-start(bf16[1024,2,128]{0,2,1:T(8,128)(2,1)} %fusion.25) | copy-start | bytes 1572868
  207.0 126.5 %all-gather.10.cloned.1.call-start = ((), (), s32[]{:S(2)}) async-start(), calls=%async_computation.4 | async-start | bytes 4718592 | tf_op jit(solution)/shard_map/all_gather | solution.py:14
Sparse Core Ops, SparseCore 0:
  10.1 76.2 all-gather.5
  90.8 94.1 all-gather.7
  207.1 31.7 reduce-scatter.1
  261.8 71.6 all-gather.9
where the time goes:
time: 393 us; the launch traced here: 392 us
  waiting for transfers between devices  199 us (51%)
  blocking collectives  79.4 us (20%)
  other arithmetic  40.9 us (10%)
  matrix products  34.7 us (9%)
  local copies, waits for them, and re-layouts  23.4 us (6%)
  between operations  13.9 us (4%)
    all_gather x2, waiting for transfers between devices, carried_in(): lax.all_gather(a.astype(kind), axis)  112 us
    all_gather x1, waiting for transfers between devices, on_device(): lax.all_gather(forward_b, 'space', axis=0, tiled=True)  87.4 us
    psum x1, blocking collectives, on_device(): fixed_forward = lax.psum(contrib, ('tm', 'space')).astype(jnp.bfloat16)  46.9 us
    all_gather x1, blocking collectives, carried_in(): lax.all_gather(a.astype(kind), axis)  32.5 us
    add x7, other arithmetic, combine(): value_l + latter[0] * value_e  28.9 us
    dot_general x1, matrix products, on_device(): jnp.einsum('hrn,rhk->nhk', block, inner_rows, preferred_element_type=jnp....  22 us
    while x4, local copies, waits for them, and re-layouts, carried_in(): return lax.fori_loop(0, ahead, one, state)  15.6 us
  transfers between devices with their start and end apart: 4, of which 3 were waited for; matrix products, arithmetic and copies ran while one was open for 4% of the time, Pallas kernels for 0%

commit v1 on v0

v1 whole, which is shorter than its diff:
```python
import functools

import jax
import jax.numpy as jnp
from jax import lax
from jax.experimental import pallas as pl
from jax.experimental.pallas import tpu as pltpu
from jax.sharding import PartitionSpec as P

TILE = 128
CHUNKS = 4
H = 2
CORES = 2
LAG = 2
F32 = jnp.float32
BF16 = jnp.bfloat16


def turned(a):
    return a.astype(F32).T


def kernel(
    times, spaces,
    weights, keep, rate, source, arrow, rhs, tip,
    out, fixed_out,
    w_v, keep_v, rate_v, rate_p, src_v, arrow_v, rhs_v, tip_v, sol_v, fix_v,
    r_v, s_out, s_in, ch_out, ch_in, f_all,
    c_f, c_out, c_in1, c_part, c_in2, ff, fixed_b,
    inner, inner_t, own_part, sib_out, sib_in, red_out, red_in,
    carr, b_out, b_in, bc_out, bc_in,
    local_sem, w_sem, rate_sem, pair_s, pair_r, ch_s, ch_r,
    x_s, sib_s, f_r, c1_s, c1_r, c2_s, c2_r, c3_s, c3_r,
    sp_s, sp_r, rd_s, rd_r, bp_s, bp_r, bc_s, bc_r, out_sem,
):
    rows = f_all.shape[2]
    step_rows = rows // CHUNKS
    fixed_total = ff.shape[1]
    share = fixed_total // times
    xs = spaces // CORES
    t = lax.axis_index("tm")
    p = lax.axis_index("space")
    x = p // CORES
    c = p % CORES
    y = t % 2
    z = t // 2
    z_total = times // 2
    partner = t + 1 - 2 * y
    sibling = p + 1 - 2 * c

    def remote(src, dst, send, recv, tm, space):
        return pltpu.make_async_remote_copy(
            src_ref=src, dst_ref=dst, send_sem=send, recv_sem=recv,
            device_id={"tm": tm, "space": space}, device_id_type=pl.DeviceIdType.MESH,
        )

    loads = [
        pltpu.make_async_copy(a, b, local_sem.at[i])
        for i, (a, b) in enumerate(
            ((source, src_v), (rate, rate_v), (keep, keep_v), (rhs, rhs_v), (tip, tip_v), (arrow, arrow_v))
        )
    ]
    for load in loads:
        load.start()

    def w_copy(h, q):
        cols = pl.ds(pl.multiple_of(q * rows, rows), rows)
        return pltpu.make_async_copy(weights.at[h, :, cols], w_v.at[h, :, cols], w_sem.at[h, q])

    barrier = pltpu.get_barrier_semaphore()

    def greet_t(d, _):
        pl.semaphore_signal(
            barrier, inc=1, device_id={"tm": (t + d) % times, "space": p},
            device_id_type=pl.DeviceIdType.MESH,
        )
        return 0

    def greet_s(d, _):
        pl.semaphore_signal(
            barrier, inc=1, device_id={"tm": t, "space": (p + d) % spaces},
            device_id_type=pl.DeviceIdType.MESH,
        )
        return 0

    lax.fori_loop(1, times, greet_t, 0)
    lax.fori_loop(1, spaces, greet_s, 0)
    for h in range(H):
        lax.fori_loop(0, p + 1, lambda q, _, h=h: (w_copy(h, q).start(), 0)[1], 0)
    loads[0].wait()
    loads[1].wait()

    def part(k):
        return pl.ds(pl.multiple_of(k * step_rows, step_rows), step_rows)

    def woven(h, k):
        return pl.ds(2 * k * step_rows + h, step_rows, stride=2)

    for h in range(H):
        for k in range(CHUNKS):
            s_out[h, part(k)] = src_v[woven(h, k), :].astype(BF16)
    pl.semaphore_wait(barrier, times - 1 + spaces - 1)

    def pair_copy(h, k):
        i = h * CHUNKS + k
        return remote(s_out.at[h, part(k)], s_in.at[h, part(k)], pair_s.at[i], pair_r.at[i], partner, p)

    rate_copy = remote(rate_v, rate_p, rate_sem.at[0], rate_sem.at[1], partner, p)
    rate_copy.start()
    for h in range(H):
        for k in range(CHUNKS):
            pair_copy(h, k).start()

    tiles = rows // TILE

    def spread(ref, parity):
        for h in range(H):
            for j in range(tiles):
                row = ref[pl.ds(h * tiles + j, 1), :]
                r_v[parity, h, pl.ds(j * TILE, TILE), :] = jnp.broadcast_to(row, (TILE, TILE)).T

    spread(rate_v, y)

    @pl.when(z == 0)
    def _():
        ch_in[...] = jnp.zeros_like(ch_in)

    @pl.when(z == z_total - 1)
    def _():
        bc_in[...] = jnp.zeros_like(bc_in)

    rate_copy.wait_recv()
    spread(rate_p, 1 - y)

    def chain_copy(h, k):
        i = h * CHUNKS + k
        return remote(
            ch_out.at[h, part(k)], ch_in.at[h, part(k)], ch_s.at[i], ch_r.at[i], (t + 2) % times, p
        )

    def x_copy(h, k, other):
        i = h * CHUNKS + k
        piece = f_all.at[h, p, part(k)]
        return remote(piece, piece, x_s.at[i, other], f_r.at[i, p], t, other * CORES + c)

    def sib_copy(h, k, from_x):
        i = h * CHUNKS + k
        q = from_x * CORES + c
        piece = f_all.at[h, q, part(k)]
        return remote(piece, piece, sib_s.at[i, from_x], f_r.at[i, q], t, sibling)

    def got(h, k, q):
        i = h * CHUNKS + k
        piece = f_all.at[h, q, part(k)]
        return remote(piece, piece, sib_s.at[i, 0], f_r.at[i, q], t, sibling)

    def scan_chunk(h, k):
        pair_copy(h, k).wait_recv()

        @pl.when(z > 0)
        def _():
            chain_copy(h, k).wait_recv()

        mine = src_v[woven(h, k), :]
        theirs = s_in[h, part(k)].astype(F32)
        s_e = jnp.where(y == 0, mine, theirs)
        s_o = jnp.where(y == 0, theirs, mine)
        f_e = s_e + r_v[0, h, part(k)] * ch_in[h, part(k)].astype(F32)
        f_o = s_o + r_v[1, h, part(k)] * f_e
        ch_out[h, part(k)] = f_o.astype(BF16)

        @pl.when(z < z_total - 1)
        def _():
            chain_copy(h, k).start()

        f_all[h, p, part(k)] = jnp.where(y == 0, f_e, f_o).astype(BF16)
        lax.fori_loop(x + 1, xs, lambda o, _: (x_copy(h, k, o).start(), 0)[1], 0)

        @pl.when(c == 0)
        def _():
            sib_copy(h, k, x).start()

    def relay(h, k):
        def one(o, _):
            got(h, k, o * CORES + c).wait_recv()
            sib_copy(h, k, o).start()
            return 0

        lax.fori_loop(0, x, one, 0)

    def scan_step(i, _):
        @pl.when(i < H * CHUNKS)
        def _():
            scan_chunk(i // CHUNKS, i % CHUNKS)

        @pl.when(i >= LAG)
        def _():
            relay((i - LAG) // CHUNKS, (i - LAG) % CHUNKS)

        return 0

    lax.fori_loop(0, H * CHUNKS + LAG, scan_step, 0)

    def ds_share(n):
        return pl.ds(pl.multiple_of(n * share, share), share)

    def c1_copy(h, d):
        to = (t + d) % times
        return remote(
            c_out.at[h, ds_share(to)], c_in1.at[h, d], c1_s.at[h, d], c1_r.at[h, d], to, p
        )

    def c2_copy(h, d):
        return remote(
            c_part.at[h], c_in2.at[h, d], c2_s.at[h, d], c2_r.at[h, d], t, (p + d) % spaces
        )

    def c3_copy(h, d):
        return remote(
            ff.at[h, ds_share(t)], ff.at[h, ds_share(t)], c3_s.at[h, d], c3_r.at[h, d],
            (t + d) % times, p,
        )

    def c3_got(h, d):
        piece = ff.at[h, ds_share((t - d + times) % times)]
        return remote(piece, piece, c3_s.at[h, d], c3_r.at[h, d], (t + d) % times, p)

    loads[3].wait()
    loads[5].wait()
    for h in range(H):
        f_t = turned(f_all[h, p]).astype(BF16)
        coupling = jnp.dot(f_t, arrow_v[h], preferred_element_type=F32).T
        c_f[h] = rhs_v[h] - coupling
        c_out[h] = c_f[h].astype(BF16)
        lax.fori_loop(1, times, lambda d, _, h=h: (c1_copy(h, d).start(), 0)[1], 0)

    def second(h):
        def add(d, acc):
            c1_copy(h, d).wait_recv()
            return acc + c_in1[h, d].astype(F32)

        c_part[h] = lax.fori_loop(1, times, add, c_f[h, ds_share(t)])
        lax.fori_loop(1, spaces, lambda d, _: (c2_copy(h, d).start(), 0)[1], 0)

    def third(h):
        def add(d, acc):
            c2_copy(h, d).wait_recv()
            return acc + c_in2[h, d]

        ff[h, ds_share(t)] = lax.fori_loop(1, spaces, add, c_part[h]).astype(BF16)
        lax.fori_loop(1, times, lambda d, _: (c3_copy(h, d).start(), 0)[1], 0)

    def tip_solve(h):
        lax.fori_loop(1, times, lambda d, _: (c3_got(h, d).wait_recv(), 0)[1], 0)
        lower = lax.broadcasted_iota(jnp.int32, (fixed_total, fixed_total), 0) >= (
            lax.broadcasted_iota(jnp.int32, (fixed_total, fixed_total), 1)
        )
        tip_l = jnp.where(lower, tip_v[h], jnp.zeros((), BF16))
        tip_in = jnp.dot(tip_l, ff[h], preferred_element_type=F32).astype(BF16)
        fixed = jnp.dot(turned(tip_in).astype(BF16), tip_l, preferred_element_type=F32).T
        fix_v[h] = fixed
        fixed_b[h] = fixed.astype(BF16)

    block = 2 * TILE

    def masked(h, b, q):
        cols = pl.ds(pl.multiple_of(q * rows, rows), rows)
        pieces = []
        for j in range(block // TILE):
            at = pl.ds(pl.multiple_of(b * block + j * TILE, TILE), TILE)
            kept = keep_v[pl.ds(b * (block // TILE) + j, 1), cols].astype(BF16)
            pieces.append(w_v[h, at, cols] * kept)
        return jnp.concatenate(pieces, axis=0), cols

    def first_product(h):
        def wait_block(q, _):
            w_copy(h, q).wait()
            relayed = ((q % CORES) == c) & (q // CORES < x)

            @pl.when((q < p) & jnp.logical_not(relayed))
            def _():
                lax.fori_loop(0, CHUNKS, lambda k, _: (got(h, k, q).wait_recv(), 0)[1], 0)

            return 0

        lax.fori_loop(0, p + 1, wait_block, 0)

        def row_block(b, _):
            at = pl.ds(pl.multiple_of(b * block, block), block)

            def below(q, acc):
                piece, cols = masked(h, b, q)
                w_v[h, at, cols] = piece
                return acc + jnp.dot(piece, f_all[h, q], preferred_element_type=F32)

            acc = lax.fori_loop(0, p, below, jnp.zeros((block, f_all.shape[3]), F32))
            piece, cols = masked(h, b, p)
            row_id = b * block + lax.broadcasted_iota(jnp.int32, (block, rows), 0)
            col_id = lax.broadcasted_iota(jnp.int32, (block, rows), 1)
            piece = jnp.where(row_id >= col_id, piece, jnp.zeros((), BF16))
            w_v[h, at, cols] = piece
            acc = acc + jnp.dot(piece, f_all[h, p], preferred_element_type=F32)
            inner[h, at] = acc.astype(BF16)
            return 0

        lax.fori_loop(0, rows // block, row_block, 0)
        inner_t[h] = turned(inner[h]).astype(BF16)

    def back(h, q, put):
        def col_block(b, _):
            cols = pl.ds(pl.multiple_of(q * rows + b * block, block), block)
            value = jnp.dot(inner_t[h], w_v[h, :, cols], preferred_element_type=F32).T
            put(pl.ds(pl.multiple_of(b * block, block), block), value)
            return 0

        lax.fori_loop(0, rows // block, col_block, 0)

    def sp_copy(h, o):
        return remote(sib_out.at[h, o], sib_in.at[h, o], sp_s.at[h, o], sp_r.at[h, o], t, sibling)

    def rd_copy(h, o):
        return remote(
            red_out.at[h, o], red_in.at[h, x], rd_s.at[h, o], rd_r.at[h, x], t, o * CORES + c
        )

    def rd_got(h, o):
        return remote(red_out.at[h, o], red_in.at[h, o], rd_s.at[h, o], rd_r.at[h, o], t, sibling)

    def second_product(h):
        def for_sibling(o, _):
            def put(at, value):
                sib_out[h, o, at] = value.astype(BF16)

            back(h, o * CORES + 1 - c, put)
            sp_copy(h, o).start()
            return 0

        lax.fori_loop(0, x + c, for_sibling, 0)

        def for_own(o, _):
            def put(at, value):
                own_part[h, o, at] = value

            back(h, o * CORES + c, put)
            return 0

        lax.fori_loop(0, x + 1, for_own, 0)

    def pass_on(h):
        def one(o, _):
            sp_copy(h, o).wait_recv()
            red_out[h, o] = (own_part[h, o] + sib_in[h, o].astype(F32)).astype(BF16)
            rd_copy(h, o).start()
            return 0

        lax.fori_loop(0, x, one, 0)

    loads[2].wait()
    first_product(0)
    second_product(0)
    second(0)
    pass_on(0)
    second(1)
    first_product(1)
    third(0)
    second_product(1)
    third(1)
    pass_on(1)
    loads[4].wait()
    tip_solve(0)
    tip_solve(1)

    def bp_copy(h, k):
        i = h * CHUNKS + k
        return remote(b_out.at[h, part(k)], b_in.at[h, part(k)], bp_s.at[i], bp_r.at[i], partner, p)

    def bc_copy(h, k):
        i = h * CHUNKS + k
        return remote(
            bc_out.at[h, part(k)], bc_in.at[h, part(k)], bc_s.at[i], bc_r.at[i],
            (t + times - 2) % times, p,
        )

    def gather_scaled(h):
        @pl.when(c == 0)
        def _():
            sp_copy(h, x).wait_recv()

        lax.fori_loop(x + 1, xs, lambda o, _: (rd_got(h, o).wait_recv(), 0)[1], 0)

        def one(k, _):
            at = part(k)
            drop = jnp.dot(arrow_v[h, at], fixed_b[h], preferred_element_type=F32)
            carr[h, at] = own_part[h, x, at] - drop

            @pl.when(c == 0)
            def _():
                carr[h, at] += sib_in[h, x, at].astype(F32)

            def more(o, _):
                carr[h, at] += red_in[h, o, at].astype(F32)
                return 0

            lax.fori_loop(x + 1, xs, more, 0)
            b_out[h, at] = carr[h, at].astype(BF16)
            bp_copy(h, k).start()
            return 0

        lax.fori_loop(0, CHUNKS, one, 0)

    def back_chunk(h, k):
        bp_copy(h, k).wait_recv()

        @pl.when(z < z_total - 1)
        def _():
            bc_copy(h, k).wait_recv()

        mine = carr[h, part(k)]
        theirs = b_in[h, part(k)].astype(F32)
        c_e = jnp.where(y == 0, mine, theirs)
        c_o = jnp.where(y == 0, theirs, mine)
        sol_o = c_o + bc_in[h, part(k)].astype(F32)
        sol_e = c_e + r_v[1, h, part(k)] * sol_o
        bc_out[h, part(k)] = (r_v[0, h, part(k)] * sol_e).astype(BF16)

        @pl.when(z > 0)
        def _():
            bc_copy(h, k).start()

        sol_v[woven(h, k), :] = jnp.where(y == 0, sol_e, sol_o)

    gather_scaled(0)
    gather_scaled(1)
    lax.fori_loop(0, H * CHUNKS, lambda i, _: (back_chunk(i // CHUNKS, i % CHUNKS), 0)[1], 0)
    out_copy = pltpu.make_async_copy(sol_v, out, out_sem.at[0])
    fix_copy = pltpu.make_async_copy(fix_v, fixed_out, out_sem.at[1])
    out_copy.start()
    fix_copy.start()

    rate_copy.wait_send()

    def drain(i, _):
        h, k = i // CHUNKS, i % CHUNKS
        pair_copy(h, k).wait_send()
        bp_copy(h, k).wait_send()

        @pl.when(z < z_total - 1)
        def _():
            chain_copy(h, k).wait_send()

        @pl.when(z > 0)
        def _():
            bc_copy(h, k).wait_send()

        lax.fori_loop(x + 1, xs, lambda o, _: (x_copy(h, k, o).wait_send(), 0)[1], 0)
        lax.fori_loop(0, x + 1 - c, lambda o, _: (sib_copy(h, k, o).wait_send(), 0)[1], 0)
        return 0

    lax.fori_loop(0, H * CHUNKS, drain, 0)

    for h in range(H):
        lax.fori_loop(1, times, lambda d, _, h=h: (c1_copy(h, d).wait_send(), 0)[1], 0)
        lax.fori_loop(1, spaces, lambda d, _, h=h: (c2_copy(h, d).wait_send(), 0)[1], 0)
        lax.fori_loop(1, times, lambda d, _, h=h: (c3_copy(h, d).wait_send(), 0)[1], 0)
        lax.fori_loop(0, x + c, lambda o, _, h=h: (sp_copy(h, o).wait_send(), 0)[1], 0)
        lax.fori_loop(0, x, lambda o, _, h=h: (rd_copy(h, o).wait_send(), 0)[1], 0)
    out_copy.wait()
    fix_copy.wait()


def on_device(times, spaces, inverse_factor, tile_mask, carry_rate, right_side, arrow_rows, fixed_rhs, tip_factor):
    rows = right_side.shape[1]
    nodes = inverse_factor.shape[3]
    k = right_side.shape[3]
    fixed_total = tip_factor.shape[1]
    xs = spaces // CORES
    share = fixed_total // times
    tile_total = tile_mask.shape[0]
    own_tiles = rows // TILE
    table = jnp.maximum(tile_mask, jnp.eye(tile_total, dtype=jnp.int32))
    own = lax.dynamic_slice_in_dim(table, lax.axis_index("space") * own_tiles, own_tiles, 0)
    keep = jnp.repeat((own > 0).astype(F32), TILE, axis=1)
    rate = carry_rate[0].T.reshape(H * own_tiles, TILE)
    source = right_side.reshape(H * rows, k)
    arrow = arrow_rows[0].transpose(1, 0, 2)
    share_rows = fixed_rhs.shape[1]
    start = lax.axis_index(("tm", "space")) * share_rows
    rhs = lax.dynamic_update_slice_in_dim(
        jnp.zeros((H, fixed_total, k), F32), fixed_rhs, start, 1
    )
    weights = inverse_factor[:, 0]
    n = H * CHUNKS
    dma = pltpu.SemaphoreType.DMA
    half = lambda *s: pltpu.VMEM(s, BF16)
    full = lambda *s: pltpu.VMEM(s, F32)
    scratch = [
        half(H, rows, nodes), full(own_tiles, nodes), full(H * own_tiles, TILE), full(H * own_tiles, TILE),
        full(H * rows, k), half(H, rows, fixed_total), full(H, fixed_total, k),
        half(H, fixed_total, fixed_total), full(H * rows, k), full(H, fixed_total, k),
        full(2, H, rows, k), half(H, rows, k), half(H, rows, k), half(H, rows, k), half(H, rows, k),
        half(H, spaces, rows, k),
        full(H, fixed_total, k), half(H, fixed_total, k), half(H, times, share, k),
        full(H, share, k), full(H, spaces, share, k), half(H, fixed_total, k), half(H, fixed_total, k),
        half(H, rows, k), half(H, k, rows), full(H, xs, rows, k),
        half(H, xs, rows, k), half(H, xs, rows, k), half(H, xs, rows, k), half(H, xs, rows, k),
        full(H, rows, k), half(H, rows, k), half(H, rows, k), half(H, rows, k), half(H, rows, k),
        dma((6,)), dma((H, spaces)), dma((2,)), dma((n,)), dma((n,)), dma((n,)), dma((n,)),
        dma((n, xs)), dma((n, xs)), dma((n, spaces)),
        dma((H, times)), dma((H, times)), dma((H, spaces)), dma((H, spaces)), dma((H, times)), dma((H, times)),
        dma((H, xs)), dma((H, xs)), dma((H, xs)), dma((H, xs)),
        dma((n,)), dma((n,)), dma((n,)), dma((n,)), dma((2,)),
    ]
    anywhere = pl.BlockSpec(memory_space=pl.ANY)
    sol, fixed = pl.pallas_call(
        functools.partial(kernel, times, spaces),
        out_shape=(
            jax.ShapeDtypeStruct((H * rows, k), F32),
            jax.ShapeDtypeStruct((H, fixed_total, k), F32),
        ),
        in_specs=[anywhere] * 7,
        out_specs=(anywhere, anywhere),
        scratch_shapes=scratch,
        compiler_params=pltpu.CompilerParams(
            collective_id=0, has_side_effects=True, vmem_limit_bytes=56 * 1024 * 1024
        ),
        cost_estimate=pl.CostEstimate(
            flops=8 * H * rows * nodes * k, bytes_accessed=2 * H * rows * nodes, transcendentals=0
        ),
    )(weights, keep, rate, source, arrow, rhs, tip_factor)
    fixed_own = lax.dynamic_slice_in_dim(fixed, start, share_rows, 1)
    return sol.reshape(1, rows, H, k), fixed_own


def solution(mesh):
    placed = (
        P(None, "tm", "space", None),
        P(),
        P("tm", "space", None),
        P("tm", "space", None, None),
        P("tm", "space", None, None),
        P(None, ("tm", "space"), None),
        P(),
    )
    return jax.shard_map(
        functools.partial(on_device, mesh.shape["tm"], mesh.shape["space"]),
        mesh=mesh,
        in_specs=placed,
        out_specs=(P("tm", "space", None, None), P(None, ("tm", "space"), None)),
        check_vma=False,
    )
```

time: 393 us -> 98.1 us (0.25)
  waiting for transfers between devices: 199 us -> 0 us
  Pallas kernels: 0 us -> 86.4 us
  blocking collectives: 79.4 us -> 0 us
  other arithmetic: 40.9 us -> 0.7 us
  matrix products: 34.7 us -> 0 us
  local copies, waits for them, and re-layouts: 23.4 us -> 9.93 us
  between operations: 13.9 us -> 0.65 us
    all_gather x3 -> x0, waiting for transfers between devices: 199 us -> none  [the longest x2 112 us: carried_in(): lax.all_gather(a.astype(kind), axis)]
    pallas_call x0 -> x1, Pallas kernels: none -> 86.4 us  [on_device(): pl.pallas_call(functools.partial(kernel, times, spaces), out_shape=(jax.S...]
    psum x1 -> x0, blocking collectives: 46.9 us -> none  [on_device(): fixed_forward = lax.psum(contrib, ('tm', 'space')).astype(jnp.bfloat16)]
    dot_general x5 -> x0, matrix products: 34.7 us -> none  [the longest x1 22 us: on_device(): jnp.einsum('hrn,rhk->nhk', block, inner_rows, preferred_element_type=jnp....]
    all_gather x1 -> x0, blocking collectives: 32.5 us -> none  [carried_in(): lax.all_gather(a.astype(kind), axis)]
    add x8 -> x0, other arithmetic: 29 us -> none  [the longest x7 28.9 us: combine(): value_l + latter[0] * value_e]
    while x4 -> x0, local copies, waits for them, and re-layouts: 15.6 us -> none  [carried_in(): return lax.fori_loop(0, ahead, one, state)]
    convert_element_type x9 -> x1, other arithmetic: 9.47 us -> 0.7 us  [on_device(): keep = jnp.repeat((own > 0).astype(F32), TILE, axis=1)]
  transfers between devices with their start and end apart: 4 -> 0, of which waited for: 3 -> 0; matrix products, arithmetic and copies ran while one was open for 4% -> 0% of each run, Pallas kernels for 0% -> 0%
where the time goes in v1:
time: 98.1 us; the launch traced here: 97.7 us
  Pallas kernels  86.4 us (88%)
  local copies, waits for them, and re-layouts  9.93 us (10%)
    pallas_call x1, Pallas kernels, on_device(): pl.pallas_call(functools.partial(kernel, times, spaces), out_shape=(jax.S...  86.4 us
    unnamed x4, local copies, waits for them, and re-layouts  5.72 us

profile of v1, /device:TPU:0, one launch (start us, length us, event | category | flops | bytes accessed | tf_op | source)
XLA Modules:
  0.0 97.7 jit_solution(7540828594166580817)
XLA Ops:
  0.6 0.7 fusion.1
  1.3 1.3 %reshape.17.rate = f32[16,128]{1,0:T(8,128)} reshape(f32[2,1024]{1,0:T(2,128)} %bitcast.15) | data formatting | bytes 16384 | tf_op jit(solution)/shard_map/reshape | solution.py:483
  2.6 0.1 copy.9
  2.7 0.7 broadcast_bitcast_fusion.keep
  3.5 0.7 constant_dynamic-update-slice_fusion.rhs
  4.2 0.0 copy-start
  4.2 3.5 %copy.12 = bf16[1,1024,2,512]{3,1,2,0:T(8,128)(2,1)} copy(bf16[1,1024,2,512]{3,2,1,0:T(2,128)(2,1)} %param.11) | data formatting | bytes 4194304 | tf_op args[4]
  7.7 0.0 copy-done
  7.7 86.4 %shard_map.86 = (f32[2048,128]{1,0:T(8,128)}, f32[2,512,128]{2,1,0:T(8,128)}) custom-call(bf16[2,1024,4096]{2,1,0:T(8,128)(2,1)} %bitcast.16, f32[8,4096]{1,0:T(8,128)} %broadcast_bitcast_fusion.keep, f32[16,128]{1,0:T(8,128)} %reshape.17.rate, f32[2048,128]{1,0:T(8,128)} %bitcast.17, bf16[2,1024,512]{2,1,0:T(8,128)(2,1)} %bitcast.13, ...), custom_call_target="tpu_custom_call" | custom-call | flops 8589934592 | bytes 16777216 | tf_op jit(solution)/shard_map/pallas_call | solution.py:514
  94.1 1.3 %constant_dynamic-slice_fusion = f32[2,16,128]{2,1,0:T(8,128)} fusion(f32[2,512,128]{2,1,0:T(8,128)} %get-tuple-element.5, s32[]{:T(128)S(6)} %select_n.8), kind=kLoop, calls=%fused_computation.7 | loop fusion | bytes 32772 | tf_op jit(solution)/shard_map/dynamic_slice | solution.py:530
  95.4 2.3 %copy.15 = f32[1,1024,2,128]{3,2,1,0:T(2,128)} copy(f32[1,1024,2,128]{3,2,1,0:T(2,128)} %bitcast.14) | data formatting | bytes 2097152
  (1 shorter events, 0.0 us)
Async XLA Ops:
  4.2 3.5 %copy-start = (f32[2,512,128]{2,1,0:T(8,128)}, f32[2,512,128]{2,1,0:T(8,128)S(1)}, u32[]{:S(2)}) copy-start(f32[2,512,128]{2,1,0:T(8,128)S(1)} %constant_dynamic-update-slice_fusion.rhs) | copy-start | bytes 1572868

commit v2 on v1

--- a/solution.py
+++ b/solution.py
@@ -24,7 +24,7 @@
     times, spaces,
     weights, keep, rate, source, arrow, rhs, tip,
     out, fixed_out,
-    w_v, keep_v, rate_v, rate_p, src_v, arrow_v, rhs_v, tip_v, sol_v, fix_v,
+    w_v, keep_v, table_v, rate_v, rate_p, src_v, arrow_3, arrow_v, rhs_v, tip_v, sol_v, fix_v,
     r_v, s_out, s_in, ch_out, ch_in, f_all,
     c_f, c_out, c_in1, c_part, c_in2, ff, fixed_b,
     inner, inner_t, own_part, sib_out, sib_in, red_out, red_in,
@@ -57,7 +57,7 @@
     loads = [
         pltpu.make_async_copy(a, b, local_sem.at[i])
         for i, (a, b) in enumerate(
-            ((source, src_v), (rate, rate_v), (keep, keep_v), (rhs, rhs_v), (tip, tip_v), (arrow, arrow_v))
+            ((source, src_v), (rate, rate_v), (keep, table_v), (rhs, rhs_v), (tip, tip_v), (arrow, arrow_3))
         )
     ]
     for load in loads:
@@ -116,7 +116,7 @@
     def spread(ref, parity):
         for h in range(H):
             for j in range(tiles):
-                row = ref[pl.ds(h * tiles + j, 1), :]
+                row = ref[pl.ds(h, 1), pl.ds(j * TILE, TILE)]
                 r_v[parity, h, pl.ds(j * TILE, TILE), :] = jnp.broadcast_to(row, (TILE, TILE)).T
 
     spread(rate_v, y)
@@ -129,6 +129,18 @@
     def _():
         bc_in[...] = jnp.zeros_like(bc_in)
 
+    loads[2].wait()
+    tile_total = table_v.shape[0]
+    own_tiles = table_v[pl.ds(pl.multiple_of(p * tiles, tiles), tiles), :]
+    tile_row = p * tiles + lax.broadcasted_iota(jnp.int32, (tiles, tile_total), 0)
+    tile_col = lax.broadcasted_iota(jnp.int32, (tiles, tile_total), 1)
+    marks = jnp.where((own_tiles > 0) | (tile_row == tile_col), 1.0, 0.0).astype(BF16)
+    hot = lax.broadcasted_iota(jnp.int32, (tile_total, tile_total * TILE), 0) == (
+        lax.broadcasted_iota(jnp.int32, (tile_total, tile_total * TILE), 1) // TILE
+    )
+    keep_v[...] = jnp.dot(
+        marks, jnp.where(hot, 1.0, 0.0).astype(BF16), preferred_element_type=F32
+    )
     rate_copy.wait_recv()
     spread(rate_p, 1 - y)
 
@@ -188,19 +200,6 @@
 
         lax.fori_loop(0, x, one, 0)
 
-    def scan_step(i, _):
-        @pl.when(i < H * CHUNKS)
-        def _():
-            scan_chunk(i // CHUNKS, i % CHUNKS)
-
-        @pl.when(i >= LAG)
-        def _():
-            relay((i - LAG) // CHUNKS, (i - LAG) % CHUNKS)
-
-        return 0
-
-    lax.fori_loop(0, H * CHUNKS + LAG, scan_step, 0)
-
     def ds_share(n):
         return pl.ds(pl.multiple_of(n * share, share), share)
 
@@ -225,14 +224,17 @@
         piece = ff.at[h, ds_share((t - d + times) % times)]
         return remote(piece, piece, c3_s.at[h, d], c3_r.at[h, d], (t + d) % times, p)
 
+    share_rows = rhs_v.shape[1]
+    own_rows = pl.ds((t * spaces + p) * share_rows, share_rows)
     loads[3].wait()
-    loads[5].wait()
-    for h in range(H):
+
+    def couple(h):
         f_t = turned(f_all[h, p]).astype(BF16)
         coupling = jnp.dot(f_t, arrow_v[h], preferred_element_type=F32).T
-        c_f[h] = rhs_v[h] - coupling
+        c_f[h] = -coupling
+        c_f[h, own_rows] += rhs_v[h]
         c_out[h] = c_f[h].astype(BF16)
-        lax.fori_loop(1, times, lambda d, _, h=h: (c1_copy(h, d).start(), 0)[1], 0)
+        lax.fori_loop(1, times, lambda d, _: (c1_copy(h, d).start(), 0)[1], 0)
 
     def second(h):
         def add(d, acc):
@@ -258,7 +260,8 @@
         tip_l = jnp.where(lower, tip_v[h], jnp.zeros((), BF16))
         tip_in = jnp.dot(tip_l, ff[h], preferred_element_type=F32).astype(BF16)
         fixed = jnp.dot(turned(tip_in).astype(BF16), tip_l, preferred_element_type=F32).T
-        fix_v[h] = fixed
+        c_f[h] = fixed
+        fix_v[h] = c_f[h, own_rows]
         fixed_b[h] = fixed.astype(BF16)
 
     block = 2 * TILE
@@ -272,7 +275,7 @@
             pieces.append(w_v[h, at, cols] * kept)
         return jnp.concatenate(pieces, axis=0), cols
 
-    def first_product(h):
+    def first_ready(h):
         def wait_block(q, _):
             w_copy(h, q).wait()
             relayed = ((q % CORES) == c) & (q // CORES < x)
@@ -285,6 +288,7 @@
 
         lax.fori_loop(0, p + 1, wait_block, 0)
 
+    def first_product(h, low, high):
         def row_block(b, _):
             at = pl.ds(pl.multiple_of(b * block, block), block)
 
@@ -303,8 +307,7 @@
             inner[h, at] = acc.astype(BF16)
             return 0
 
-        lax.fori_loop(0, rows // block, row_block, 0)
-        inner_t[h] = turned(inner[h]).astype(BF16)
+        lax.fori_loop(low, high, row_block, 0)
 
     def back(h, q, put):
         def col_block(b, _):
@@ -326,7 +329,7 @@
     def rd_got(h, o):
         return remote(red_out.at[h, o], red_in.at[h, o], rd_s.at[h, o], rd_r.at[h, o], t, sibling)
 
-    def second_product(h):
+    def second_product(h, low, sib_high, own_high):
         def for_sibling(o, _):
             def put(at, value):
                 sib_out[h, o, at] = value.astype(BF16)
@@ -335,7 +338,7 @@
             sp_copy(h, o).start()
             return 0
 
-        lax.fori_loop(0, x + c, for_sibling, 0)
+        lax.fori_loop(low, sib_high, for_sibling, 0)
 
         def for_own(o, _):
             def put(at, value):
@@ -344,7 +347,7 @@
             back(h, o * CORES + c, put)
             return 0
 
-        lax.fori_loop(0, x + 1, for_own, 0)
+        lax.fori_loop(low, own_high, for_own, 0)
 
     def pass_on(h):
         def one(o, _):
@@ -355,20 +358,58 @@
 
         lax.fori_loop(0, x, one, 0)
 
-    loads[2].wait()
-    first_product(0)
-    second_product(0)
+    row_blocks = rows // block
+    first_at = H * CHUNKS + LAG - row_blocks
+
+    def scan_step(i, _):
+        @pl.when(i < H * CHUNKS)
+        def _():
+            scan_chunk(i // CHUNKS, i % CHUNKS)
+
+        @pl.when(i < CHUNKS)
+        def _():
+            at = part(i)
+            for h in range(H):
+                arrow_v[h, at] = arrow_3[at, h, :]
+
+        @pl.when(i >= LAG)
+        def _():
+            relay((i - LAG) // CHUNKS, (i - LAG) % CHUNKS)
+
+        for h in range(H):
+            @pl.when(i == CHUNKS * (h + 1))
+            def _():
+                couple(h)
+
+        @pl.when(i == first_at)
+        def _():
+            first_ready(0)
+
+        @pl.when(i >= first_at)
+        def _():
+            first_product(0, i - first_at, i - first_at + 1)
+
+        return 0
+
+    loads[5].wait()
+    lax.fori_loop(0, H * CHUNKS + LAG, scan_step, 0)
+
+    def far(h):
+        inner_t[h] = turned(inner[h]).astype(BF16)
+        second_product(h, 0, x, x)
+        pass_on(h)
+
+    def near(h):
+        second_product(h, x, x + c, x + 1)
+
     second(0)
-    pass_on(0)
+    far(0)
+    third(0)
+    near(0)
     second(1)
-    first_product(1)
-    third(0)
-    second_product(1)
-    third(1)
-    pass_on(1)
+    first_ready(1)
+    first_product(1, 0, row_blocks)
     loads[4].wait()
-    tip_solve(0)
-    tip_solve(1)
 
     def bp_copy(h, k):
         i = h * CHUNKS + k
@@ -429,9 +470,15 @@
 
         sol_v[woven(h, k), :] = jnp.where(y == 0, sol_e, sol_o)
 
+    tip_solve(0)
     gather_scaled(0)
+    far(1)
+    third(1)
+    near(1)
+    lax.fori_loop(0, CHUNKS, lambda k, _: (back_chunk(0, k), 0)[1], 0)
+    tip_solve(1)
     gather_scaled(1)
-    lax.fori_loop(0, H * CHUNKS, lambda i, _: (back_chunk(i // CHUNKS, i % CHUNKS), 0)[1], 0)
+    lax.fori_loop(0, CHUNKS, lambda k, _: (back_chunk(1, k), 0)[1], 0)
     out_copy = pltpu.make_async_copy(sol_v, out, out_sem.at[0])
     fix_copy = pltpu.make_async_copy(fix_v, fixed_out, out_sem.at[1])
     out_copy.start()
@@ -477,26 +524,19 @@
     share = fixed_total // times
     tile_total = tile_mask.shape[0]
     own_tiles = rows // TILE
-    table = jnp.maximum(tile_mask, jnp.eye(tile_total, dtype=jnp.int32))
-    own = lax.dynamic_slice_in_dim(table, lax.axis_index("space") * own_tiles, own_tiles, 0)
-    keep = jnp.repeat((own > 0).astype(F32), TILE, axis=1)
-    rate = carry_rate[0].T.reshape(H * own_tiles, TILE)
+    rate = carry_rate[0].T
     source = right_side.reshape(H * rows, k)
-    arrow = arrow_rows[0].transpose(1, 0, 2)
+    arrow = arrow_rows[0]
     share_rows = fixed_rhs.shape[1]
-    start = lax.axis_index(("tm", "space")) * share_rows
-    rhs = lax.dynamic_update_slice_in_dim(
-        jnp.zeros((H, fixed_total, k), F32), fixed_rhs, start, 1
-    )
     weights = inverse_factor[:, 0]
     n = H * CHUNKS
     dma = pltpu.SemaphoreType.DMA
     half = lambda *s: pltpu.VMEM(s, BF16)
     full = lambda *s: pltpu.VMEM(s, F32)
     scratch = [
-        half(H, rows, nodes), full(own_tiles, nodes), full(H * own_tiles, TILE), full(H * own_tiles, TILE),
-        full(H * rows, k), half(H, rows, fixed_total), full(H, fixed_total, k),
-        half(H, fixed_total, fixed_total), full(H * rows, k), full(H, fixed_total, k),
+        half(H, rows, nodes), full(own_tiles, nodes), pltpu.VMEM((tile_total, tile_total), jnp.int32), full(H, rows), full(H, rows),
+        full(H * rows, k), half(rows, H, fixed_total), half(H, rows, fixed_total), full(H, share_rows, k),
+        half(H, fixed_total, fixed_total), full(H * rows, k), full(H, share_rows, k),
         full(2, H, rows, k), half(H, rows, k), half(H, rows, k), half(H, rows, k), half(H, rows, k),
         half(H, spaces, rows, k),
         full(H, fixed_total, k), half(H, fixed_total, k), half(H, times, share, k),
@@ -515,7 +555,7 @@
         functools.partial(kernel, times, spaces),
         out_shape=(
             jax.ShapeDtypeStruct((H * rows, k), F32),
-            jax.ShapeDtypeStruct((H, fixed_total, k), F32),
+            jax.ShapeDtypeStruct((H, share_rows, k), F32),
         ),
         in_specs=[anywhere] * 7,
         out_specs=(anywhere, anywhere),
@@ -526,9 +566,8 @@
         cost_estimate=pl.CostEstimate(
             flops=8 * H * rows * nodes * k, bytes_accessed=2 * H * rows * nodes, transcendentals=0
         ),
-    )(weights, keep, rate, source, arrow, rhs, tip_factor)
-    fixed_own = lax.dynamic_slice_in_dim(fixed, start, share_rows, 1)
-    return sol.reshape(1, rows, H, k), fixed_own
+    )(weights, tile_mask, rate, source, arrow, fixed_rhs, tip_factor)
+    return sol.reshape(1, rows, H, k), fixed
 
 
 def solution(mesh):

time: 98.1 us -> 89 us (0.907)
  local copies, waits for them, and re-layouts: 9.93 us -> 3.59 us
  Pallas kernels: 86.4 us -> 84.5 us
    unnamed x4 -> x2, local copies, waits for them, and re-layouts: 5.72 us -> 3.59 us
    reshape x2 -> x0, local copies, waits for them, and re-layouts: 2.04 us -> none  [the longest x1 1.3 us: on_device(): rate = carry_rate[0].T.reshape(H * own_tiles, TILE)]
    pallas_call x1, Pallas kernels: 86.4 us -> 84.5 us  [on_device(): pl.pallas_call(functools.partial(kernel, times, spaces), out_shape=(jax.S...]
    dynamic_slice x1 -> x0, local copies, waits for them, and re-layouts: 1.34 us -> none  [on_device(): fixed_own = lax.dynamic_slice_in_dim(fixed, start, share_rows, 1)]
where the time goes in v2:
time: 89 us; the launch traced here: 88.7 us
  Pallas kernels  84.5 us (95%)
  local copies, waits for them, and re-layouts  3.59 us (4%)
    pallas_call x1, Pallas kernels, on_device(): pl.pallas_call(functools.partial(kernel, times, spaces), out_shape=(jax.S...  84.5 us
    unnamed x2, local copies, waits for them, and re-layouts  3.59 us

profile of v2, /device:TPU:0, one launch (start us, length us, event | category | flops | bytes accessed | tf_op | source)
XLA Modules:
  0.0 88.7 jit_solution(14587954515212431544)
XLA Ops:
  0.6 84.5 %shard_map.86 = (f32[2048,128]{1,0:T(8,128)}, f32[2,16,128]{2,1,0:T(8,128)}) custom-call(bf16[2,1024,4096]{2,1,0:T(8,128)(2,1)} %bitcast.8, s32[32,32]{1,0:T(8,128)} %keep.1, f32[2,1024]{1,0:T(2,128)} %bitcast.11, f32[2048,128]{1,0:T(8,128)} %bitcast.10, bf16[1024,2,512]{2,1,0:T(2,128)(2,1)} %bitcast.9, f32[2,16,128]{2,1,0:T(8,128)} %rhs.1, ...), custom_call_target="tpu_custom_call" | custom-call | flops 8589934592 | bytes 16777216 | tf_op jit(solution)/shard_map/pallas_call | solution.py:554
  85.2 2.3 %copy.11 = f32[1,1024,2,128]{3,2,1,0:T(2,128)} copy(f32[1,1024,2,128]{3,2,1,0:T(2,128)} %bitcast.7) | data formatting | bytes 2097152
  87.4 1.3 %copy.12 = f32[2,16,128]{2,1,0:T(8,128)} copy(f32[2,16,128]{2,1,0:T(8,128)} %get-tuple-element.9) | data formatting | bytes 32768

commit v3 on v2

--- a/solution.py
+++ b/solution.py
@@ -8,7 +8,7 @@
 from jax.sharding import PartitionSpec as P
 
 TILE = 128
-CHUNKS = 4
+CHUNKS = 8
 H = 2
 CORES = 2
 LAG = 2
@@ -359,7 +359,7 @@
         lax.fori_loop(0, x, one, 0)
 
     row_blocks = rows // block
-    first_at = H * CHUNKS + LAG - row_blocks
+    first_at = CHUNKS + LAG
 
     def scan_step(i, _):
         @pl.when(i < H * CHUNKS)
@@ -385,7 +385,7 @@
         def _():
             first_ready(0)
 
-        @pl.when(i >= first_at)
+        @pl.when((i >= first_at) & (i < first_at + row_blocks))
         def _():
             first_product(0, i - first_at, i - first_at + 1)
 
@@ -513,6 +513,15 @@
         lax.fori_loop(0, x, lambda o, _, h=h: (rd_copy(h, o).wait_send(), 0)[1], 0)
     out_copy.wait()
     fix_copy.wait()
+
+
+def hand_over(sol, fixed, sol_out, fixed_out, sems):
+    one = pltpu.make_async_copy(sol, sol_out, sems.at[0])
+    two = pltpu.make_async_copy(fixed, fixed_out, sems.at[1])
+    one.start()
+    two.start()
+    one.wait()
+    two.wait()
 
 
 def on_device(times, spaces, inverse_factor, tile_mask, carry_rate, right_side, arrow_rows, fixed_rhs, tip_factor):
@@ -567,6 +576,14 @@
             flops=8 * H * rows * nodes * k, bytes_accessed=2 * H * rows * nodes, transcendentals=0
         ),
     )(weights, tile_mask, rate, source, arrow, fixed_rhs, tip_factor)
+    sol, fixed = pl.pallas_call(
+        hand_over,
+        out_shape=(jax.ShapeDtypeStruct(sol.shape, F32), jax.ShapeDtypeStruct(fixed.shape, F32)),
+        in_specs=[anywhere] * 2,
+        out_specs=(anywhere, anywhere),
+        scratch_shapes=[dma((2,))],
+        cost_estimate=pl.CostEstimate(flops=0, bytes_accessed=2 * sol.size * 4, transcendentals=0),
+    )(sol, fixed)
     return sol.reshape(1, rows, H, k), fixed
 
 

time: 89 us -> 115 us (1.29)
  Pallas kernels: 84.5 us -> 114 us
  local copies, waits for them, and re-layouts: 3.59 us -> 0 us
    pallas_call x0 -> x1, Pallas kernels: none -> 33.4 us  [on_device(): pl.pallas_call(hand_over, out_shape=(jax.ShapeDtypeStruct(sol.shape, F32)...]
    pallas_call x1, Pallas kernels: 84.5 us -> 80.7 us  [on_device(): pl.pallas_call(functools.partial(kernel, times, spaces), out_shape=(jax.S...]
    unnamed x2 -> x0, local copies, waits for them, and re-layouts: 3.59 us -> none
where the time goes in v3:
time: 115 us
  Pallas kernels  114 us (99%)
    pallas_call x1, Pallas kernels, on_device(): pl.pallas_call(functools.partial(kernel, times, spaces), out_shape=(jax.S...  80.7 us
    pallas_call x1, Pallas kernels, on_device(): pl.pallas_call(hand_over, out_shape=(jax.ShapeDtypeStruct(sol.shape, F32)...  33.4 us

profile of v3, /device:TPU:0, one launch (start us, length us, event | category | flops | bytes accessed | tf_op | source)
XLA Modules:
  0.0 114.8 jit_solution(596769153122871355)
XLA Ops:
  0.6 80.7 %shard_map.86 = (f32[2048,128]{1,0:T(8,128)}, f32[2,16,128]{2,1,0:T(8,128)}) custom-call(bf16[2,1024,4096]{2,1,0:T(8,128)(2,1)} %bitcast.7, s32[32,32]{1,0:T(8,128)} %keep.1, f32[2,1024]{1,0:T(2,128)} %bitcast.11, f32[2048,128]{1,0:T(8,128)} %bitcast.9, bf16[1024,2,512]{2,1,0:T(2,128)(2,1)} %bitcast.8, f32[2,16,128]{2,1,0:T(8,128)} %rhs.1, ...), custom_call_target="tpu_custom_call" | custom-call | flops 8589934592 | bytes 16777216 | tf_op jit(solution)/shard_map/pallas_call | solution.py:563
  81.4 33.4 %shard_map.87 = (f32[2048,128]{1,0:T(8,128)}, f32[2,16,128]{2,1,0:T(8,128)}) custom-call(f32[2048,128]{1,0:T(8,128)} %get-tuple-element.6.sol, f32[2,16,128]{2,1,0:T(8,128)} %get-tuple-element.7.fixed), custom_call_target="tpu_custom_call" | custom-call | bytes 2097152 | tf_op jit(solution)/shard_map/pallas_call | solution.py:579

commit v4 on v3

--- a/solution.py
+++ b/solution.py
@@ -309,56 +309,46 @@
 
         lax.fori_loop(low, high, row_block, 0)
 
-    def back(h, q, put):
-        def col_block(b, _):
-            cols = pl.ds(pl.multiple_of(q * rows + b * block, block), block)
-            value = jnp.dot(inner_t[h], w_v[h, :, cols], preferred_element_type=F32).T
-            put(pl.ds(pl.multiple_of(b * block, block), block), value)
-            return 0
-
-        lax.fori_loop(0, rows // block, col_block, 0)
-
-    def sp_copy(h, o):
-        return remote(sib_out.at[h, o], sib_in.at[h, o], sp_s.at[h, o], sp_r.at[h, o], t, sibling)
-
-    def rd_copy(h, o):
-        return remote(
-            red_out.at[h, o], red_in.at[h, x], rd_s.at[h, o], rd_r.at[h, x], t, o * CORES + c
-        )
-
-    def rd_got(h, o):
-        return remote(red_out.at[h, o], red_in.at[h, o], rd_s.at[h, o], rd_r.at[h, o], t, sibling)
-
-    def second_product(h, low, sib_high, own_high):
-        def for_sibling(o, _):
-            def put(at, value):
-                sib_out[h, o, at] = value.astype(BF16)
-
-            back(h, o * CORES + 1 - c, put)
-            sp_copy(h, o).start()
-            return 0
-
-        lax.fori_loop(low, sib_high, for_sibling, 0)
-
-        def for_own(o, _):
-            def put(at, value):
-                own_part[h, o, at] = value
-
-            back(h, o * CORES + c, put)
-            return 0
-
-        lax.fori_loop(low, own_high, for_own, 0)
-
-    def pass_on(h):
-        def one(o, _):
-            sp_copy(h, o).wait_recv()
-            red_out[h, o] = (own_part[h, o] + sib_in[h, o].astype(F32)).astype(BF16)
-            rd_copy(h, o).start()
-            return 0
-
-        lax.fori_loop(0, x, one, 0)
-
     row_blocks = rows // block
+
+    def span(b):
+        return pl.ds(pl.multiple_of(b * block, block), block)
+
+    def back(h, q, b):
+        cols = pl.ds(pl.multiple_of(q * rows + b * block, block), block)
+        return jnp.dot(inner_t[h], w_v[h, :, cols], preferred_element_type=F32).T
+
+    def sp_copy(h, o, b):
+        n = o * row_blocks + b
+        return remote(
+            sib_out.at[h, o, span(b)], sib_in.at[h, o, span(b)], sp_s.at[h, n], sp_r.at[h, n], t, sibling
+        )
+
+    def rd_copy(h, o, b):
+        return remote(
+            red_out.at[h, o, span(b)], red_in.at[h, x, span(b)], rd_s.at[h, o * row_blocks + b],
+            rd_r.at[h, x * row_blocks + b], t, o * CORES + c,
+        )
+
+    def rd_got(h, o, b):
+        n = o * row_blocks + b
+        return remote(
+            red_out.at[h, o, span(b)], red_in.at[h, o, span(b)], rd_s.at[h, n], rd_r.at[h, n], t, sibling
+        )
+
+    def for_sibling(h, o, b):
+        sib_out[h, o, span(b)] = back(h, o * CORES + 1 - c, b).astype(BF16)
+        sp_copy(h, o, b).start()
+
+    def for_own(h, o, b):
+        own_part[h, o, span(b)] = back(h, o * CORES + c, b)
+
+    def pass_on(h, o, b):
+        sp_copy(h, o, b).wait_recv()
+        total = own_part[h, o, span(b)] + sib_in[h, o, span(b)].astype(F32)
+        red_out[h, o, span(b)] = total.astype(BF16)
+        rd_copy(h, o, b).start()
+
     first_at = CHUNKS + LAG
 
     def scan_step(i, _):
@@ -396,11 +386,32 @@
 
     def far(h):
         inner_t[h] = turned(inner[h]).astype(BF16)
-        second_product(h, 0, x, x)
-        pass_on(h)
+        count = x * row_blocks
+
+        def one(i, _):
+            @pl.when(i < count)
+            def _():
+                for_sibling(h, i // row_blocks, i % row_blocks)
+                for_own(h, i // row_blocks, i % row_blocks)
+
+            @pl.when(i >= 1)
+            def _():
+                pass_on(h, (i - 1) // row_blocks, (i - 1) % row_blocks)
+
+            return 0
+
+        lax.fori_loop(0, count + jnp.minimum(x, 1), one, 0)
 
     def near(h):
-        second_product(h, x, x + c, x + 1)
+        def one(b, _):
+            @pl.when(c == 1)
+            def _():
+                for_sibling(h, x, b)
+
+            for_own(h, x, b)
+            return 0
+
+        lax.fori_loop(0, row_blocks, one, 0)
 
     second(0)
     far(0)
@@ -423,14 +434,19 @@
         )
 
     def gather_scaled(h):
-        @pl.when(c == 0)
-        def _():
-            sp_copy(h, x).wait_recv()
-
-        lax.fori_loop(x + 1, xs, lambda o, _: (rd_got(h, o).wait_recv(), 0)[1], 0)
+        per = CHUNKS // row_blocks
 
         def one(k, _):
             at = part(k)
+
+            @pl.when(k % per == 0)
+            def _():
+                @pl.when(c == 0)
+                def _():
+                    sp_copy(h, x, k // per).wait_recv()
+
+                lax.fori_loop(x + 1, xs, lambda o, _: (rd_got(h, o, k // per).wait_recv(), 0)[1], 0)
+
             drop = jnp.dot(arrow_v[h, at], fixed_b[h], preferred_element_type=F32)
             carr[h, at] = own_part[h, x, at] - drop
 
@@ -509,19 +525,21 @@
         lax.fori_loop(1, times, lambda d, _, h=h: (c1_copy(h, d).wait_send(), 0)[1], 0)
         lax.fori_loop(1, spaces, lambda d, _, h=h: (c2_copy(h, d).wait_send(), 0)[1], 0)
         lax.fori_loop(1, times, lambda d, _, h=h: (c3_copy(h, d).wait_send(), 0)[1], 0)
-        lax.fori_loop(0, x + c, lambda o, _, h=h: (sp_copy(h, o).wait_send(), 0)[1], 0)
-        lax.fori_loop(0, x, lambda o, _, h=h: (rd_copy(h, o).wait_send(), 0)[1], 0)
+        lax.fori_loop(
+            0, (x + c) * row_blocks,
+            lambda i, _, h=h: (sp_copy(h, i // row_blocks, i % row_blocks).wait_send(), 0)[1], 0,
+        )
+        lax.fori_loop(
+            0, x * row_blocks,
+            lambda i, _, h=h: (rd_copy(h, i // row_blocks, i % row_blocks).wait_send(), 0)[1], 0,
+        )
     out_copy.wait()
     fix_copy.wait()
 
 
-def hand_over(sol, fixed, sol_out, fixed_out, sems):
-    one = pltpu.make_async_copy(sol, sol_out, sems.at[0])
-    two = pltpu.make_async_copy(fixed, fixed_out, sems.at[1])
-    one.start()
-    two.start()
-    one.wait()
-    two.wait()
+def hand_over(sol, fixed, sol_out, fixed_out):
+    sol_out[...] = sol[...]
+    fixed_out[...] = fixed[...]
 
 
 def on_device(times, spaces, inverse_factor, tile_mask, carry_rate, right_side, arrow_rows, fixed_rhs, tip_factor):
@@ -556,7 +574,7 @@
         dma((6,)), dma((H, spaces)), dma((2,)), dma((n,)), dma((n,)), dma((n,)), dma((n,)),
         dma((n, xs)), dma((n, xs)), dma((n, spaces)),
         dma((H, times)), dma((H, times)), dma((H, spaces)), dma((H, spaces)), dma((H, times)), dma((H, times)),
-        dma((H, xs)), dma((H, xs)), dma((H, xs)), dma((H, xs)),
+        *[dma((H, xs * rows // (2 * TILE)))] * 4,
         dma((n,)), dma((n,)), dma((n,)), dma((n,)), dma((2,)),
     ]
     anywhere = pl.BlockSpec(memory_space=pl.ANY)
@@ -579,9 +597,15 @@
     sol, fixed = pl.pallas_call(
         hand_over,
         out_shape=(jax.ShapeDtypeStruct(sol.shape, F32), jax.ShapeDtypeStruct(fixed.shape, F32)),
-        in_specs=[anywhere] * 2,
-        out_specs=(anywhere, anywhere),
-        scratch_shapes=[dma((2,))],
+        grid=(2,),
+        in_specs=[
+            pl.BlockSpec((sol.shape[0] // 2, k), lambda i: (i, 0)),
+            pl.BlockSpec((1,) + fixed.shape[1:], lambda i: (i, 0, 0)),
+        ],
+        out_specs=(
+            pl.BlockSpec((sol.shape[0] // 2, k), lambda i: (i, 0)),
+            pl.BlockSpec((1,) + fixed.shape[1:], lambda i: (i, 0, 0)),
+        ),
         cost_estimate=pl.CostEstimate(flops=0, bytes_accessed=2 * sol.size * 4, transcendentals=0),
     )(sol, fixed)
     return sol.reshape(1, rows, H, k), fixed

time: 115 us -> 84.6 us (0.74)
  the two profiles are of different devices: /device:TPU:0 before, /device:TPU:2 now
where the time goes in v4:
time: 84.6 us; the launch traced here: 84.4 us
  Pallas kernels  83.7 us (99%)
    pallas_call x1, Pallas kernels, on_device(): pl.pallas_call(functools.partial(kernel, times, spaces), out_shape=(jax.S...  81.7 us
    pallas_call x1, Pallas kernels, on_device(): pl.pallas_call(hand_over, out_shape=(jax.ShapeDtypeStruct(sol.shape, F32)...  2.07 us

profile of v4, /device:TPU:2, one launch (start us, length us, event | category | flops | bytes accessed | tf_op | source)
XLA Modules:
  0.0 84.4 jit_solution(4344086009433294692)
XLA Ops:
  0.6 81.7 %shard_map.86 = (f32[2048,128]{1,0:T(8,128)}, f32[2,16,128]{2,1,0:T(8,128)}) custom-call(bf16[2,1024,4096]{2,1,0:T(8,128)(2,1)} %bitcast.7, s32[32,32]{1,0:T(8,128)} %keep.1, f32[2,1024]{1,0:T(2,128)} %bitcast.11, f32[2048,128]{1,0:T(8,128)} %bitcast.9, bf16[1024,2,512]{2,1,0:T(2,128)(2,1)} %bitcast.8, f32[2,16,128]{2,1,0:T(8,128)} %rhs.1, ...), custom_call_target="tpu_custom_call" | custom-call | flops 8589934592 | bytes 16777216 | tf_op jit(solution)/shard_map/pallas_call | solution.py:581
  82.3 2.1 %shard_map.87 = (f32[2048,128]{1,0:T(8,128)}, f32[2,16,128]{2,1,0:T(8,128)}) custom-call(f32[2048,128]{1,0:T(8,128)} %get-tuple-element.6.sol, f32[2,16,128]{2,1,0:T(8,128)} %get-tuple-element.7.fixed), custom_call_target="tpu_custom_call" | custom-call | bytes 2097152 | tf_op jit(solution)/shard_map/pallas_call | solution.py:597
